TPU v7x, 512 devices: a whole 4x4x16 slice. The times are simulated.
512 devices in a mesh: pipe: 4 (over y), seq: 16 (over z), tensor: 8 (over x, core).
Axes of the slice: x: 4, y: 4, z: 16, core: 2. Of those that a mesh axis runs over, the one named last changes fastest.
Arguments:
- layer_input: bfloat16 [4, 2048, 8192], P('pipe', 'seq', 'tensor'), may hold values from -320 to 320
- conv_out: bfloat16 [4, 2048, 8192], P('pipe', 'seq', 'tensor'), may hold values from -8 to 8
- act_grad: bfloat16 [4, 2048, 8192], P('pipe', 'seq', 'tensor'), may hold values from -6 to 6
- conv_kernel: bfloat16 [4, 4, 8192], P('pipe', None, 'tensor'), may hold values from -3 to 3
- in_proj: bfloat16 [4, 8192, 8192], P('pipe', 'seq', 'tensor'), may hold values from -0.0625 to 0.0625
- sketch_matrix: bfloat16 [4, 8192, 512], P('pipe', 'tensor'), may hold values from -0.0625 to 0.0625
Outputs:
- passed_grad: bfloat16 [4, 2048, 8192], P('pipe', 'tensor', 'seq')
- basis: bfloat16 [4, 8192, 512], P('pipe', 'tensor')
All inputs are finite; a program needn't handle non-finite values.
Results may differ from a plain program's by a relative error of at most 0.017.
Values may be sent and summed in bfloat16 or wider, within the bound.
No kernel may reach another device: no remote copies, remote signals or barrier semaphores. Data moves between devices by JAX's collectives and lax.ppermute only.
A program may use at most 64 MiB of HBM per device.

v0:
```python
import math
import jax
import jax.numpy as jnp
from jax import lax
from jax.sharding import PartitionSpec as P

D = 8192


def passed_along(block, axis, distance):
    devices = range(lax.axis_size(axis))
    route = [(i - distance, i) for i in devices if i - distance in devices]
    return lax.ppermute(block, axis, route)


def shifted(value, axis, by):
    count = lax.axis_size(axis)
    return lax.ppermute(value, axis, [(i, (i + by) % count) for i in range(count)])


def finish_basis(sketch, gram):
    low = jnp.linalg.cholesky(gram)
    ortho_t = lax.linalg.triangular_solve(low, sketch.T, left_side=True, lower=True)
    return (ortho_t.T * math.sqrt(D)).astype(jnp.bfloat16)


def local(layer_input, conv_out, act_grad, conv_kernel, in_proj, sketch_matrix):
    acts = layer_input[0]
    kernel = conv_kernel[0]
    weights = in_proj[0]
    test_matrix = sketch_matrix[0]
    tok_rows = acts.shape[0]
    taps = kernel.shape[0]
    pval = conv_out[0].astype(jnp.float32)
    sig = jax.nn.sigmoid(pval)
    pre_grad = act_grad[0].astype(jnp.float32) * sig * (1.0 + pval * (1.0 - sig))
    ahead = passed_along(pre_grad[: taps - 1], "seq", -1)
    extended = jnp.concatenate([pre_grad, ahead], axis=0)
    total = jnp.zeros(pre_grad.shape, jnp.float32)
    for tap in range(taps):
        total = total + kernel[tap].astype(jnp.float32) * extended[tap : tap + tok_rows]
    in_grad = total.astype(jnp.bfloat16)
    partial_grad = lax.dot_general(
        lax.all_gather(in_grad, "seq", axis=0, tiled=True),
        weights,
        (((1,), (1,)), ((), ())),
        preferred_element_type=jnp.float32,
    )
    input_grad = lax.psum_scatter(
        partial_grad.astype(jnp.bfloat16), "tensor", scatter_dimension=0, tiled=True
    )
    passed = shifted(input_grad, "pipe", -1)
    row_terms = jnp.dot(in_grad, test_matrix, preferred_element_type=jnp.float32)
    sketch_rows = lax.psum(row_terms, "tensor").astype(jnp.bfloat16)
    sketch_part = lax.dot_general(
        acts, sketch_rows, (((0,), (0,)), ((), ())), preferred_element_type=jnp.float32
    )
    sketch = lax.psum(sketch_part, "seq")
    gram_part = jnp.dot(sketch.T, sketch, precision=lax.Precision.HIGHEST)
    gram = lax.psum(gram_part, "tensor")
    basis = finish_basis(sketch, gram)
    return (passed[None], basis[None])


def solution(mesh):
    placed = (
        P("pipe", "seq", "tensor"),
        P("pipe", "seq", "tensor"),
        P("pipe", "seq", "tensor"),
        P("pipe", None, "tensor"),
        P("pipe", "seq", "tensor"),
        P("pipe", "tensor", None),
    )
    return jax.shard_map(
        local,
        mesh=mesh,
        in_specs=placed,
        out_specs=(P("pipe", "tensor", "seq"), P("pipe", "tensor", None)),
        check_vma=False,
    )
```

profile of v0, /device:TPU:26, one launch (start us, length us, event | category | flops | bytes accessed | tf_op | source)
XLA Modules:
  0.0 470.1 jit_solution(17740369245081746752)
XLA Ops:
  7.2 1.4 fusion.30
  8.7 1.3 collective-permute-start
  10.0 0.9 slice_convert_fusion.3
  10.8 3.5 collective-permute-done
  14.9 24.3 %all-reduce.8 = bf16[128,512]{1,0:T(8,128)(2,1)S(1)} all-reduce(f32[128,512]{1,0:T(8,128)S(1)} %fusion.15), channel_id=1, replica_groups=mesh['pipe'=4,'seq'=16,'tensor'=8] {'tensor'}, use_global_device_ids=true, to_apply=%region_1.0 | all-reduce | flops 65536 | bytes 393216 | tf_op jit(solution)/shard_map/psum | solution.py:54
  39.2 1.8 convolution_bitcast_fusion
  41.0 149.0 %all-reduce.5.cloned.1.call-done = f32[1024,512]{0,1:T(8,128)} async-done(((f32[1024,512]{0,1:T(8,128)}), f32[1024,512]{0,1:T(8,128)}) %all-reduce.5.cloned.1.call-update) | async-done | bytes 2097168 | tf_op jit(solution)/shard_map/psum | solution.py:58
  190.0 6.7 %fusion.56 = f32[512,512]{0,1:T(8,128)} fusion(f32[1024,512]{0,1:T(8,128)} %all-reduce.5.cloned.1.call-done), kind=kOutput, calls=%fused_computation.103 | convolution fusion | flops 3221225472 | bytes 3145728 | tf_op jit(solution)/shard_map/dot_general | solution.py:59
  196.8 0.7 all-gather.2.cloned.1.call-update
  198.0 70.5 %all-reduce.7.cloned.1.call-done = f32[512,512]{0,1:T(8,128)} async-done(((f32[512,512]{0,1:T(8,128)}), f32[512,512]{0,1:T(8,128)}) %all-reduce.7.cloned.1.call-update) | async-done | bytes 1048592 | tf_op jit(solution)/shard_map/psum | solution.py:60
  268.5 1.6 copy.9
  270.4 1.0 copy-done.7
  271.4 11.7 %cholesky.104 = f32[128,128]{1,0:T(8,128)S(1)} custom-call(f32[128,128]{1,0:T(8,128)S(1)} %cholesky.266), custom_call_target="Cholesky" | custom-call | tf_op jit(solution)/shard_map/jit(cholesky)/cholesky | solution.py:22
  283.3 9.8 %custom-call.30 = f32[1,128,128]{1,2,0:T(8,128)S(1)} custom-call(f32[1,128,128]{2,1,0:T(8,128)S(1)} %get-tuple-element.31), custom_call_target="InvertDiagBlocksLowerTriangular" | custom-call | tf_op jit(solution)/shard_map/jit(cholesky)/cholesky | solution.py:22
  293.1 1.2 constant_dynamic-update-slice_fusion.3
  294.4 1.3 convolution_subtract_fusion.2
  295.6 11.7 %cholesky.217 = f32[128,128]{1,0:T(8,128)S(1)} custom-call(f32[128,128]{1,0:T(8,128)S(1)} %cholesky.270), custom_call_target="Cholesky" | custom-call | tf_op jit(solution)/shard_map/jit(cholesky)/cholesky | solution.py:22
  307.4 10.0 %custom-call.31 = f32[1,128,128]{1,2,0:T(8,128)S(1)} custom-call(f32[1,128,128]{2,1,0:T(8,128)S(1)} %get-tuple-element.28), custom_call_target="InvertDiagBlocksLowerTriangular" | custom-call | tf_op jit(solution)/shard_map/jit(cholesky)/cholesky | solution.py:22
  317.6 1.4 convolution_subtract_fusion.3
  319.1 11.7 %cholesky.238 = f32[128,128]{1,0:T(8,128)S(1)} custom-call(f32[128,128]{1,0:T(8,128)S(1)} %cholesky.275), custom_call_target="Cholesky" | custom-call | tf_op jit(solution)/shard_map/jit(cholesky)/cholesky | solution.py:22
  330.8 21.4 %all-gather.2.cloned.1.call-done = bf16[2048,1024]{1,0:T(8,128)(2,1)} async-done(((bf16[128,1024]{1,0:T(8,128)(2,1)}), bf16[2048,1024]{1,0:T(8,128)(2,1)}) %all-gather.2.cloned.1.call-update) | async-done | bytes 4194320 | tf_op jit(solution)/shard_map/all_gather | solution.py:44
  352.2 5.9 %convolution_convert_fusion = bf16[2048,512]{1,0:T(8,128)(2,1)} fusion(bf16[2048,1024]{1,0:T(8,128)(2,1)} %all-gather.2.cloned.1.call-done, bf16[1,512,1024]{2,1,0:T(8,128)(2,1)S(1)} %copy-done), kind=kOutput, calls=%fused_computation.2 | convolution fusion | flops 2148532224 | bytes 7340032 | tf_op jit(solution)/shard_map/dot_general | solution.py:43
  358.1 0.6 select_reduce_fusion.1
  358.8 9.8 %custom-call.32 = f32[1,128,128]{1,2,0:T(8,128)S(1)} custom-call(f32[1,128,128]{2,1,0:T(8,128)S(1)} %get-tuple-element.25), custom_call_target="InvertDiagBlocksLowerTriangular" | custom-call | tf_op jit(solution)/shard_map/jit(cholesky)/cholesky | solution.py:22
  368.6 0.8 convolution_dynamic-update-slice_fusion.1
  369.4 1.5 convolution_subtract_fusion.4
  370.9 11.9 %cholesky.255 = f32[128,128]{1,0:T(8,128)S(1)} custom-call(f32[128,128]{1,0:T(8,128)S(1)} %convolution_subtract_fusion.4), custom_call_target="Cholesky" | custom-call | tf_op jit(solution)/shard_map/jit(cholesky)/cholesky | solution.py:22
  382.8 0.6 compare_reduce_fusion.2
  384.8 0.6 compare_reduce_fusion.1
  386.1 0.6 select_reduce_fusion
  386.7 0.6 compare_reduce_fusion
  388.0 2.3 select_select_fusion
  390.3 13.6 %while.1 = (s32[]{:T(128)}, f32[512,512]{1,0:T(8,128)}, s32[4,2]{0,1:T(2,128)S(1)}, f32[4,128,128]{2,1,0:T(8,128)}, s32[]{:T(128)}) while((s32[]{:T(128)}, f32[512,512]{1,0:T(8,128)}, s32[4,2]{0,1:T(2,128)S(1)}, f32[4,128,128]{2,1,0:T(8,128)}, s32[]{:T(128)}) %tuple.35), condition=%wide.while_cond, body=%wide.while_body.sunk | while | flops 2 | bytes 132205 | solution.py:23
  390.9 2.8 bitcast_dynamic-update-slice_fusion.2
  394.4 2.8 bitcast_dynamic-update-slice_fusion.2
  397.8 2.8 bitcast_dynamic-update-slice_fusion.2
  401.2 2.8 bitcast_dynamic-update-slice_fusion.2
  404.0 40.1 %custom-call.33 = f32[4,128,128]{1,2,0:T(8,128)S(1)} custom-call(f32[4,128,128]{2,1,0:T(8,128)} %get-tuple-element.9), custom_call_target="InvertDiagBlocksLowerTriangular" | custom-call | tf_op jit(solution)/shard_map/triangular_solve | solution.py:23
  444.8 1.5 convolution_subtract_fusion.1
  446.9 1.8 convolution_subtract_fusion
  449.4 0.8 copy-done.5
  450.1 2.8 fusion.7
  453.0 2.4 collective-permute-start.1
  455.4 1.7 fusion.44
  457.1 1.6 fusion.10
  458.8 1.3 copy.10
  460.1 2.6 collective-permute-done.1
  462.7 0.7 copy.32
  (53 shorter events, 6.3 us)
Async XLA Ops:
  7.2 345.0 %copy-start = (bf16[1,512,1024]{2,1,0:T(8,128)(2,1)S(1)}, bf16[1,512,1024]{2,1,0:T(8,128)(2,1)}, u32[]{:S(2)}) copy-start(bf16[1,512,1024]{2,1,0:T(8,128)(2,1)} %param.10) | copy-start | bytes 3145732
  7.2 7.4 %copy-start.9 = (bf16[1,1024,512]{2,1,0:T(8,128)(2,1)S(1)}, bf16[1,1024,512]{2,1,0:T(8,128)(2,1)}, u32[]{:S(2)}) copy-start(bf16[1,1024,512]{2,1,0:T(8,128)(2,1)} %param.11) | copy-start | bytes 3145732
  7.2 32.0 %copy-start.10 = (bf16[1,128,1024]{2,1,0:T(8,128)(2,1)S(1)}, bf16[1,128,1024]{2,1,0:T(8,128)(2,1)}, u32[]{:S(2)}) copy-start(bf16[1,128,1024]{2,1,0:T(8,128)(2,1)} %param.6) | copy-start | bytes 786436
  7.2 182.8 %all-reduce.5.cloned.1.call-start = ((), (), s32[]{:S(2)}) async-start(), calls=%async_computation.3 | async-start | bytes 4194304 | tf_op jit(solution)/shard_map/psum | solution.py:58
  8.7 5.6 %collective-permute-start = (f32[3,1024]{1,0:T(4,128)S(1)}, f32[3,1024]{1,0:T(4,128)S(1)}, u32[]{:S(2)}, u32[]{:S(2)}) collective-permute-start(f32[3,1024]{1,0:T(4,128)S(1)} %slice.150), channel_id=1, source_target_pairs={{8,0},{16,8},{24,16},{32,24},{40,32},{48,40},{56,48},{64,56},{72,6... | collective-permute-start | bytes 36872 | tf_op jit(solution)/shard_map/ppermute | solution.py:13
  14.5 26.4 %copy-start.8 = (bf16[128,1024]{1,0:T(8,128)(2,1)}, bf16[128,1024]{1,0:T(8,128)(2,1)S(1)}, u32[]{:S(2)}) copy-start(bf16[128,1024]{1,0:T(8,128)(2,1)S(1)} %fusion.22) | copy-start | bytes 786436
  41.0 227.5 %all-reduce.7.cloned.1.call-start = ((), (), s32[]{:S(2)}) async-start(), calls=%async_computation.4 | async-start | bytes 2097152 | tf_op jit(solution)/shard_map/psum | solution.py:60
  196.8 155.4 %all-gather.2.cloned.1.call-start = ((), (), s32[]{:S(2)}) async-start(), calls=%async_computation.1 | async-start | bytes 4456448 | tf_op jit(solution)/shard_map/all_gather | solution.py:44
  197.5 255.5 %reduce-scatter.2.cloned.1.call-start = ((), (), s32[]{:S(2)}) async-start(), calls=%async_computation.2 | async-start | bytes 2359296 | tf_op jit(solution)/shard_map/reduce_scatter | solution.py:49
  268.5 1.7 copy-start.6
  270.4 1.0 copy-start.7
  317.6 40.5 %copy-start.4 = (f32[512,512]{1,0:T(8,128)}, f32[512,512]{1,0:T(8,128)S(1)}, u32[]{:S(2)}) copy-start(f32[512,512]{1,0:T(8,128)S(1)} %convolution_dynamic-update-slice_fusion) | copy-start | bytes 3145732
  358.1 86.0 %copy-start.1 = (f32[1024,512]{0,1:T(8,128)S(1)}, f32[1024,512]{0,1:T(8,128)}, u32[]{:S(2)}) copy-start(f32[1024,512]{0,1:T(8,128)} %all-reduce.5.cloned.1.call-done) | copy-start | bytes 6291460
  444.8 4.6 copy-start.2
  446.9 2.4 copy-start.3
  449.3 0.8 copy-start.5
  453.0 9.7 %collective-permute-start.1 = (bf16[256,512]{1,0:T(8,128)(2,1)}, bf16[256,512]{1,0:T(8,128)(2,1)S(1)}, u32[]{:S(2)}, u32[]{:S(2)}) collective-permute-start(bf16[256,512]{1,0:T(8,128)(2,1)} %reduce-scatter.2.cloned.1.call-done), channel_id=1, source_target_pairs={{0,384},{128,0},{256,128},{384,256},{1,385},{129,1},{257,129},{385... | collective-permute-start | bytes 786440 | tf_op jit(solution)/shard_map/ppermute | solution.py:18
Sparse Core Ops, SparseCore 0:
  41.1 148.8 all-reduce.4
  196.9 71.6 all-reduce.6
  271.2 80.9 all-gather.1
  358.2 33.6 reduce-scatter.1
where the time goes:
time: 475 us; the launch traced here: 470 us
  waiting for transfers between devices  248 us (52%)
  other arithmetic  127 us (27%)
  matrix products  30.9 us (7%)
  blocking collectives  24.3 us (5%)
  local copies, waits for them, and re-layouts  19.3 us (4%)
  between operations  17 us (4%)
    psum x1, waiting for transfers between devices, local(): sketch = lax.psum(sketch_part, 'seq')  149 us
    another operation x14, other arithmetic, finish_basis(): low = jnp.linalg.cholesky(gram)  79.9 us
    psum x1, waiting for transfers between devices, local(): gram = lax.psum(gram_part, 'tensor')  70.5 us
    another operation x3, other arithmetic, finish_basis(): lax.linalg.triangular_solve(low, sketch.T, left_side=True, lower=True)  42.5 us
    psum x1, blocking collectives, local(): sketch_rows = lax.psum(row_terms, 'tensor').astype(jnp.bfloat16)  24.3 us
    all_gather x1, waiting for transfers between devices, local(): lax.all_gather(in_grad, 'seq', axis=0, tiled=True)  21.4 us
    another operation x12, local copies, waits for them, and re-layouts  13.6 us
    another operation x7, matrix products, finish_basis(): lax.linalg.triangular_solve(low, sketch.T, left_side=True, lower=True)  9.66 us
  transfers between devices with their start and end apart: 6, of which 5 were waited for; matrix products, arithmetic and copies ran while one was open for 34% of the time, Pallas kernels for 0%

commit v1 on v0

--- a/solution.py
+++ b/solution.py
@@ -41,7 +41,9 @@
         total = total + kernel[tap].astype(jnp.float32) * extended[tap : tap + tok_rows]
     in_grad = total.astype(jnp.bfloat16)
     partial_grad = lax.dot_general(
-        lax.all_gather(in_grad, "seq", axis=0, tiled=True),
+        jnp.concatenate(
+            lax.all_to_all(jnp.stack([in_grad] * lax.axis_size("seq")), "seq", 0, 0), axis=0
+        ),
         weights,
         (((1,), (1,)), ((), ())),
         preferred_element_type=jnp.float32,

time: 475 us -> 573 us (1.21)
  the two profiles are of different devices: /device:TPU:26 before, /device:TPU:31 now
where the time goes in v1:
time: 573 us; the launch traced here: 568 us
  waiting for transfers between devices  324 us (57%)
  other arithmetic  127 us (22%)
  matrix products  30.8 us (5%)
  blocking collectives  27.4 us (5%)
  local copies, waits for them, and re-layouts  22.1 us (4%)
  starting transfers between devices  19.2 us (3%)
  between operations  16.9 us (3%)
    psum x1, waiting for transfers between devices, local(): sketch = lax.psum(sketch_part, 'seq')  236 us
    psum x1, waiting for transfers between devices, local(): gram = lax.psum(gram_part, 'tensor')  81 us
    another operation x14, other arithmetic, finish_basis(): low = jnp.linalg.cholesky(gram)  79.9 us
    another operation x3, other arithmetic, finish_basis(): lax.linalg.triangular_solve(low, sketch.T, left_side=True, lower=True)  42.5 us
    psum x1, blocking collectives, local(): sketch_rows = lax.psum(row_terms, 'tensor').astype(jnp.bfloat16)  27.4 us
    all_to_all x1, starting transfers between devices, local(): lax.all_to_all(jnp.stack([in_grad] * lax.axis_size('seq')), 'seq', 0, 0)  14.9 us
    another operation x12, local copies, waits for them, and re-layouts  14 us
  transfers between devices with their start and end apart: 6, of which 4 were waited for; matrix products, arithmetic and copies ran while one was open for 29% of the time, Pallas kernels for 0%

profile of v1, /device:TPU:31, one launch (start us, length us, event | category | flops | bytes accessed | tf_op | source)
XLA Modules:
  0.0 567.5 jit_solution(11140465451942483790)
XLA Ops:
  7.2 1.3 fusion.30
  8.5 1.3 collective-permute-start
  9.8 0.9 slice_convert_fusion.3
  10.7 2.5 collective-permute-done
  13.4 2.5 stack.2
  15.9 14.9 %all-to-all-start = ((bf16[16,128,1024]{2,1,0:T(8,128)(2,1)}), bf16[16,128,1024]{2,1,0:T(8,128)(2,1)}, u32[]{:S(2)}, u32[]{:S(2)}) async-start(bf16[16,128,1024]{2,1,0:T(8,128)(2,1)} %stack.2), calls=%async_computation | async-start | bytes 8388608 | tf_op jit(solution)/shard_map/all_to_all | solution.py:45
  31.2 27.4 %all-reduce.8 = bf16[128,512]{1,0:T(8,128)(2,1)S(1)} all-reduce(f32[128,512]{1,0:T(8,128)S(1)} %fusion.15), channel_id=1, replica_groups=mesh['pipe'=4,'seq'=16,'tensor'=8] {'tensor'}, use_global_device_ids=true, to_apply=%region_1.0 | all-reduce | flops 65536 | bytes 393216 | tf_op jit(solution)/shard_map/psum | solution.py:56
  58.7 1.8 convolution_bitcast_fusion
  60.5 236.5 %all-reduce.5.cloned.1.call-done = f32[1024,512]{0,1:T(8,128)} async-done(((f32[1024,512]{0,1:T(8,128)}), f32[1024,512]{0,1:T(8,128)}) %all-reduce.5.cloned.1.call-update) | async-done | bytes 2097168 | tf_op jit(solution)/shard_map/psum | solution.py:60
  297.0 6.7 %fusion.56 = f32[512,512]{0,1:T(8,128)} fusion(f32[1024,512]{0,1:T(8,128)} %all-reduce.5.cloned.1.call-done), kind=kOutput, calls=%fused_computation.103 | convolution fusion | flops 3221225472 | bytes 3145728 | tf_op jit(solution)/shard_map/dot_general | solution.py:61
  304.3 81.0 %all-reduce.7.cloned.1.call-done = f32[512,512]{0,1:T(8,128)} async-done(((f32[512,512]{0,1:T(8,128)}), f32[512,512]{0,1:T(8,128)}) %all-reduce.7.cloned.1.call-update) | async-done | bytes 1048592 | tf_op jit(solution)/shard_map/psum | solution.py:62
  385.3 1.6 copy.9
  387.2 1.0 copy-done.7
  388.2 11.7 %cholesky.104 = f32[128,128]{1,0:T(8,128)S(1)} custom-call(f32[128,128]{1,0:T(8,128)S(1)} %cholesky.266), custom_call_target="Cholesky" | custom-call | tf_op jit(solution)/shard_map/jit(cholesky)/cholesky | solution.py:22
  400.0 9.8 %custom-call.30 = f32[1,128,128]{1,2,0:T(8,128)S(1)} custom-call(f32[1,128,128]{2,1,0:T(8,128)S(1)} %get-tuple-element.31), custom_call_target="InvertDiagBlocksLowerTriangular" | custom-call | tf_op jit(solution)/shard_map/jit(cholesky)/cholesky | solution.py:22
  409.9 1.2 constant_dynamic-update-slice_fusion.3
  411.1 1.3 convolution_subtract_fusion.2
  412.4 11.7 %cholesky.217 = f32[128,128]{1,0:T(8,128)S(1)} custom-call(f32[128,128]{1,0:T(8,128)S(1)} %cholesky.270), custom_call_target="Cholesky" | custom-call | tf_op jit(solution)/shard_map/jit(cholesky)/cholesky | solution.py:22
  424.1 10.0 %custom-call.31 = f32[1,128,128]{1,2,0:T(8,128)S(1)} custom-call(f32[1,128,128]{2,1,0:T(8,128)S(1)} %get-tuple-element.28), custom_call_target="InvertDiagBlocksLowerTriangular" | custom-call | tf_op jit(solution)/shard_map/jit(cholesky)/cholesky | solution.py:22
  434.4 1.4 convolution_subtract_fusion.3
  435.8 11.7 %cholesky.238 = f32[128,128]{1,0:T(8,128)S(1)} custom-call(f32[128,128]{1,0:T(8,128)S(1)} %cholesky.275), custom_call_target="Cholesky" | custom-call | tf_op jit(solution)/shard_map/jit(cholesky)/cholesky | solution.py:22
  447.6 5.9 %convolution_convert_fusion = bf16[2048,512]{1,0:T(8,128)(2,1)} fusion(bf16[2048,1024]{1,0:T(8,128)(2,1)} %bitcast.7, bf16[1,512,1024]{2,1,0:T(8,128)(2,1)S(1)} %copy-done), kind=kOutput, calls=%fused_computation.2 | convolution fusion | flops 2148532224 | bytes 7340032 | tf_op jit(solution)/shard_map/dot_general | solution.py:43
  453.5 0.7 select_reduce_fusion.1
  454.2 9.8 %custom-call.32 = f32[1,128,128]{1,2,0:T(8,128)S(1)} custom-call(f32[1,128,128]{2,1,0:T(8,128)S(1)} %get-tuple-element.25), custom_call_target="InvertDiagBlocksLowerTriangular" | custom-call | tf_op jit(solution)/shard_map/jit(cholesky)/cholesky | solution.py:22
  464.0 0.8 convolution_dynamic-update-slice_fusion.1
  464.8 1.4 convolution_subtract_fusion.4
  466.2 11.9 %cholesky.255 = f32[128,128]{1,0:T(8,128)S(1)} custom-call(f32[128,128]{1,0:T(8,128)S(1)} %convolution_subtract_fusion.4), custom_call_target="Cholesky" | custom-call | tf_op jit(solution)/shard_map/jit(cholesky)/cholesky | solution.py:22
  478.1 0.6 compare_reduce_fusion.2
  480.0 0.6 compare_reduce_fusion.1
  481.3 0.6 select_reduce_fusion
  481.9 0.6 compare_reduce_fusion
  483.2 2.3 select_select_fusion
  485.5 14.0 %while.1 = (s32[]{:T(128)}, f32[512,512]{1,0:T(8,128)}, s32[4,2]{0,1:T(2,128)S(1)}, f32[4,128,128]{2,1,0:T(8,128)}, s32[]{:T(128)}) while((s32[]{:T(128)}, f32[512,512]{1,0:T(8,128)}, s32[4,2]{0,1:T(2,128)S(1)}, f32[4,128,128]{2,1,0:T(8,128)}, s32[]{:T(128)}) %tuple.35), condition=%wide.while_cond, body=%wide.while_body.sunk | while | flops 2 | bytes 132205 | solution.py:23
  486.2 2.9 bitcast_dynamic-update-slice_fusion.2
  489.7 2.9 bitcast_dynamic-update-slice_fusion.2
  493.2 2.9 bitcast_dynamic-update-slice_fusion.2
  496.7 2.8 bitcast_dynamic-update-slice_fusion.2
  499.5 40.1 %custom-call.33 = f32[4,128,128]{1,2,0:T(8,128)S(1)} custom-call(f32[4,128,128]{2,1,0:T(8,128)} %get-tuple-element.9), custom_call_target="InvertDiagBlocksLowerTriangular" | custom-call | tf_op jit(solution)/shard_map/triangular_solve | solution.py:23
  540.3 1.5 convolution_subtract_fusion.1
  542.4 1.8 convolution_subtract_fusion
  544.9 0.8 copy-done.5
  545.7 2.8 fusion.7
  548.5 2.4 collective-permute-start.1
  551.0 1.7 fusion.44
  552.6 1.6 fusion.10
  554.3 1.3 copy.10
  555.6 4.5 collective-permute-done.1
  560.1 0.7 copy.32
  (51 shorter events, 6.5 us)
Async XLA Ops:
  7.2 440.4 %copy-start = (bf16[1,512,1024]{2,1,0:T(8,128)(2,1)S(1)}, bf16[1,512,1024]{2,1,0:T(8,128)(2,1)}, u32[]{:S(2)}) copy-start(bf16[1,512,1024]{2,1,0:T(8,128)(2,1)} %param.10) | copy-start | bytes 3145732
  8.5 4.7 collective-permute-start
  15.9 15.0 %copy-start.8 = (bf16[1,1024,512]{2,1,0:T(8,128)(2,1)S(1)}, bf16[1,1024,512]{2,1,0:T(8,128)(2,1)}, u32[]{:S(2)}) copy-start(bf16[1,1024,512]{2,1,0:T(8,128)(2,1)} %param.11) | copy-start | bytes 3145732
  15.9 431.6 %all-to-all-start = ((bf16[16,128,1024]{2,1,0:T(8,128)(2,1)}), bf16[16,128,1024]{2,1,0:T(8,128)(2,1)}, u32[]{:S(2)}, u32[]{:S(2)}) async-start(bf16[16,128,1024]{2,1,0:T(8,128)(2,1)} %stack.2), calls=%async_computation | async-start | bytes 8388608 | tf_op jit(solution)/shard_map/all_to_all | solution.py:45
  30.9 27.8 %copy-start.9 = (bf16[1,128,1024]{2,1,0:T(8,128)(2,1)S(1)}, bf16[1,128,1024]{2,1,0:T(8,128)(2,1)}, u32[]{:S(2)}) copy-start(bf16[1,128,1024]{2,1,0:T(8,128)(2,1)} %param.6) | copy-start | bytes 786436
  30.9 266.2 %all-reduce.5.cloned.1.call-start = ((), (), s32[]{:S(2)}) async-start(), calls=%async_computation.3 | async-start | bytes 4194304 | tf_op jit(solution)/shard_map/psum | solution.py:60
  60.5 324.8 %all-reduce.7.cloned.1.call-start = ((), (), s32[]{:S(2)}) async-start(), calls=%async_computation.4 | async-start | bytes 2097152 | tf_op jit(solution)/shard_map/psum | solution.py:62
  303.8 244.7 %reduce-scatter.2.cloned.1.call-start = ((), (), s32[]{:S(2)}) async-start(), calls=%async_computation.2 | async-start | bytes 2359296 | tf_op jit(solution)/shard_map/reduce_scatter | solution.py:51
  385.3 1.7 copy-start.6
  387.2 1.0 copy-start.7
  434.4 19.1 %copy-start.4 = (f32[512,512]{1,0:T(8,128)}, f32[512,512]{1,0:T(8,128)S(1)}, u32[]{:S(2)}) copy-start(f32[512,512]{1,0:T(8,128)S(1)} %convolution_dynamic-update-slice_fusion) | copy-start | bytes 3145732
  453.5 86.1 %copy-start.1 = (f32[1024,512]{0,1:T(8,128)S(1)}, f32[1024,512]{0,1:T(8,128)}, u32[]{:S(2)}) copy-start(f32[1024,512]{0,1:T(8,128)} %all-reduce.5.cloned.1.call-done) | copy-start | bytes 6291460
  540.3 4.6 copy-start.2
  542.4 2.4 copy-start.3
  544.9 0.8 copy-start.5
  548.5 11.6 %collective-permute-start.1 = (bf16[256,512]{1,0:T(8,128)(2,1)}, bf16[256,512]{1,0:T(8,128)(2,1)S(1)}, u32[]{:S(2)}, u32[]{:S(2)}) collective-permute-start(bf16[256,512]{1,0:T(8,128)(2,1)} %reduce-scatter.2.cloned.1.call-done), channel_id=1, source_target_pairs={{0,384},{128,0},{256,128},{384,256},{1,385},{129,1},{257,129},{385... | collective-permute-start | bytes 786440 | tf_op jit(solution)/shard_map/ppermute | solution.py:18
Sparse Core Ops, SparseCore 0:
  60.6 236.3 all-reduce.4
  303.9 81.3 all-reduce.6
  453.6 40.2 reduce-scatter.1
